TPU v7x, 512 devices: a whole 4x8x8 slice. The times are simulated.
512 devices in a mesh: row: 4 (over z_hi), col: 64 (over z_lo, x, y), section: 2 (over core).
Axes of the slice: x: 4, y: 8, z: 8 (z_hi: 4, z_lo: 2; z = z_hi * 2 + z_lo), core: 2. Of those that a mesh axis runs over, the one named last changes fastest.
Arguments:
- block_vals: bfloat16 [512, 4, 512, 512], P(('row', 'col', 'section')), may hold values from 0.0099487305 to 1
- present: int32 [512, 4], P(('row', 'col', 'section')), may hold values 0 or 1
- kept_rows: int32 [512, 2], replicated, may hold values from 0 to 3, as said below
- column_owner: int32 [262144, 1], P(('row', 'col', 'section')), may hold values from 0 to 127; in each aligned block of 512 rows (0 to 511, 512 to 1023, ...) at most 8 rows name the same one
Outputs:
- pruned: bfloat16 [4, 128, 128, 8, 1024], P('row', ('col', 'section'))
- arrived: int32 [4, 128, 128, 8], P('row', ('col', 'section'))
Inputs may be any that keep to these rules, and one draw needn't show every extreme that they name: kept_rows[J, 0] is the block column's own position J // 128; kept_rows[J, 1] is another position of its cluster. `column_owner`: among the 512 matrix columns of one block column at most 8 have the same owner, and in every draw some owner receives exactly 8 from some block column.
All inputs are finite; a program needn't handle non-finite values. No bound on the sum of `present` on one device may be relied on, other than what follows from the above.
Results may differ from a plain program's by a relative error of at most 0.02.
Values may be sent and summed in bfloat16 or wider, within the bound.
No kernel may reach another device: no remote copies, remote signals or barrier semaphores. Data moves between devices by JAX's collectives and lax.ppermute only.
A program may use at most 64 MiB of HBM per device.

v0:
```python
import jax
import jax.numpy as jnp
from jax import lax
from jax.sharding import PartitionSpec as P


def shards(block_vals, present, kept_rows, column_owner):
    block_size = block_vals.shape[-1]
    blocks = block_vals.shape[1]
    kept_count = kept_rows.shape[1]
    position = lax.axis_index("row")
    cluster = lax.axis_index("col") * lax.axis_size("section") + lax.axis_index("section")
    clusters = lax.axis_size("col") * lax.axis_size("section")
    capacity = block_size // lax.axis_size("col")
    positions = jnp.arange(blocks, dtype=jnp.int32)
    live_mask = jnp.logical_or(present[0] > 0, positions == position)
    own_column = jnp.where(live_mask[:, None, None], block_vals[0], jnp.zeros_like(block_vals[0]))
    members = positions * clusters + cluster
    kept_local = jnp.take(kept_rows, members, axis=0)
    right_tiles = lax.all_to_all(own_column, "row", split_axis=0, concat_axis=0, tiled=True)
    left_blocks = jnp.take(own_column, kept_local.reshape(-1), axis=0).reshape(
        1 * lax.axis_size("row"), kept_count, block_size, block_size
    )
    expanded = lax.psum_scatter(
        jnp.einsum(
            "jmik,jke->jemi", left_blocks, right_tiles, preferred_element_type=jnp.float32
        ).astype(jnp.bfloat16),
        "row",
        scatter_dimension=0,
        tiled=True,
    ).astype(jnp.float32)[0]
    inflated = expanded * expanded
    column_mean = jnp.mean(inflated, axis=(1, 2)) + 1e-06
    columns = (
        (inflated / column_mean[:, None, None])
        .astype(jnp.bfloat16)
        .reshape(block_size, kept_count * block_size)
    )
    owners = column_owner[:, 0]
    owner_hits = (owners[:, None] == jnp.arange(clusters, dtype=jnp.int32)[None, :]).astype(
        jnp.int32
    )
    earlier = jnp.cumsum(owner_hits, axis=0) - owner_hits
    order_in = jnp.sum(earlier * owner_hits, axis=1)
    slot_of = owners * capacity + order_in
    source = (
        jnp.full((clusters * capacity,), -1, jnp.int32)
        .at[slot_of]
        .set(jnp.arange(block_size, dtype=jnp.int32))
    )
    filled = source >= 0
    picked = jnp.where(
        filled[:, None],
        jnp.take(columns, jnp.maximum(source, 0), axis=0),
        jnp.zeros((), jnp.bfloat16),
    )
    column_ids = jnp.where(filled, (position * clusters + cluster) * block_size + source, -1)
    arrived_vals, arrived_ids = (
        lax.all_to_all(
            picked.reshape(clusters, capacity, -1),
            ("col", "section"),
            split_axis=0,
            concat_axis=0,
            tiled=True,
        ),
        lax.all_to_all(
            column_ids.reshape(clusters, capacity),
            ("col", "section"),
            split_axis=0,
            concat_axis=0,
            tiled=True,
        ),
    )
    return (
        arrived_vals.reshape(1, 1, clusters, capacity, kept_count * block_size),
        arrived_ids.reshape(1, 1, clusters, capacity),
    )


def solution(mesh):
    placed = (
        P(("row", "col", "section"), None, None, None),
        P(("row", "col", "section"), None),
        P(),
        P(("row", "col", "section"), None),
    )
    return jax.shard_map(
        shards,
        mesh=mesh,
        in_specs=placed,
        out_specs=(
            P("row", ("col", "section"), None, None, None),
            P("row", ("col", "section"), None, None),
        ),
        check_vma=False,
    )
```

profile of v0, /device:TPU:1, one launch (start us, length us, event | category | flops | bytes accessed | tf_op | source)
XLA Modules:
  0.0 248.0 jit_solution(16712535934064437100)
XLA Ops:
  7.2 0.0 copy-start.2
  7.2 2.8 %copy.20 = bf16[1,4,512,512]{2,3,1,0:T(8,128)(2,1)S(1)} copy(bf16[1,4,512,512]{3,2,1,0:T(8,128)(2,1)} %param.4) | data formatting | bytes 4194304 | tf_op args[0]
  10.0 0.0 copy-done.2
  10.0 1.5 bitcast_select_fusion.1
  11.5 0.0 copy-start.1
  11.5 11.0 %all-to-all-start = ((bf16[4,512,512]{1,2,0:T(8,128)(2,1)}), bf16[4,512,512]{1,2,0:T(8,128)(2,1)S(1)}, u32[]{:S(2)}, u32[]{:S(2)}) async-start(bf16[4,512,512]{1,2,0:T(8,128)(2,1)} %bitcast_select_fusion.1), calls=%async_computation | async-start | bytes 4194304 | tf_op jit(solution)/shard_map/all_to_all | solution.py:20
  22.5 0.0 reduce-scatter.2.cloned.1.call-start
  22.5 0.0 copy-done.1
  22.5 0.1 copy.21
  22.7 0.6 gather_fusion
  23.3 0.1 compare_and_fusion
  23.4 0.1 select_n.87
  23.5 4.3 %gather_fusion.1 = bf16[8,512,512]{1,2,0:T(8,128)(2,1)} fusion(bf16[4,512,512]{1,2,0:T(8,128)(2,1)} %bitcast_select_fusion.1, s32[1024]{0:T(1024)S(1)} %pad_clamp_fusion), kind=kCustom, calls=%fused_computation.1 | custom fusion | bytes 8388640 | tf_op jit(solution)/shard_map/jit(_take)/gather | solution.py:21
  27.8 7.3 %copy.22 = bf16[4,2,512,512]{3,2,1,0:T(8,128)(2,1)} copy(bf16[4,2,512,512]{2,3,1,0:T(8,128)(2,1)} %bitcast.39) | data formatting | bytes 8388608 | tf_op jit(solution)/shard_map/jit(_take)/gather | solution.py:21
  35.1 20.0 %all-to-all-done = bf16[4,512,512]{1,2,0:T(8,128)(2,1)S(1)} async-done(((bf16[4,512,512]{1,2,0:T(8,128)(2,1)}), bf16[4,512,512]{1,2,0:T(8,128)(2,1)S(1)}, u32[]{:S(2)}, u32[]{:S(2)}) %all-to-all-start) | async-done | bytes 2097184 | tf_op jit(solution)/shard_map/all_to_all | solution.py:20
  55.1 6.6 %fusion.3 = bf16[4,512,2,512]{3,1,2,0:T(8,128)(2,1)} fusion(bf16[4,2,512,512]{3,2,1,0:T(8,128)(2,1)} %copy.22, pred[4,2]{1,0:T(4,128)(4,1)S(1)} %get-tuple-element.6, bf16[4,512,512]{1,2,0:T(8,128)(2,1)S(1)} %all-to-all-done), kind=kOutput, calls=%fused_computation.7 | convolution fusion | flops 2151677952 | bytes 10485768 | tf_op jit(solution)/shard_map/jmik,jke->jemi/dot_general | solution.py:25
  61.6 0.0 copy-start
  61.6 0.0 reduce-scatter.2.cloned.1.call-update
  61.7 0.6 copy-done
  62.3 0.1 copy.18
  62.4 0.2 fusion.12
  62.7 0.2 fusion.11
  63.0 2.4 scatter_custom_fusion
  65.5 0.7 all_to_all.14
  66.2 30.4 %all-to-all-start.2 = ((s32[128,1,8]{2,1,0:T(1,128)}), s32[128,1,8]{2,1,0:T(1,128)S(1)}, u32[]{:S(2)}, u32[]{:S(2)}) async-start(s32[128,1,8]{2,1,0:T(1,128)} %bitcast.17), calls=%async_computation.3 | async-start | bytes 131072 | tf_op jit(solution)/shard_map/all_to_all | solution.py:66
  96.6 0.1 broadcast_in_dim.66
  96.7 0.1 broadcast_in_dim.68
  96.8 69.1 %reduce-scatter.2.cloned.1.call-done = bf16[1,512,2,512]{3,1,2,0:T(8,128)(2,1)} async-done(((bf16[4,512,2,512]{3,1,2,0:T(8,128)(2,1)}), bf16[1,512,2,512]{3,1,2,0:T(8,128)(2,1)}) %reduce-scatter.2.cloned.1.call-update) | async-done | bytes 1048592 | tf_op jit(solution)/shard_map/reduce_scatter | solution.py:24
  165.9 1.5 fusion.9
  167.4 1.8 copy.23
  169.2 1.9 copy.24
  171.1 0.3 divide_convert_fusion
  171.4 4.1 %gather_fusion.2 = bf16[1024,1024]{1,0:T(8,128)(2,1)S(1)} fusion(bf16[512,1024]{1,0:T(8,128)(2,1)S(1)} %divide_convert_fusion, s32[1024]{0:T(1024)S(1)} %get-tuple-element.11), kind=kCustom, calls=%fused_computation.2 | custom fusion | bytes 4198400 | tf_op jit(solution)/shard_map/jit(_take)/gather | solution.py:54
  175.5 1.6 fusion.7
  177.1 0.0 all-to-all-done.2
  177.1 11.9 %all-to-all-start.1 = ((bf16[128,8,1024]{2,1,0:T(8,128)(2,1)}), bf16[128,8,1024]{2,1,0:T(8,128)(2,1)S(1)}, u32[]{:S(2)}, u32[]{:S(2)}) async-start(bf16[128,8,1024]{2,1,0:T(8,128)(2,1)} %fusion.7), calls=%async_computation.2 | async-start | bytes 4194304 | tf_op jit(solution)/shard_map/all_to_all | solution.py:59
  189.0 0.7 copy.26
  189.6 50.2 %all-to-all-done.1 = bf16[128,8,1024]{2,1,0:T(8,128)(2,1)S(1)} async-done(((bf16[128,8,1024]{2,1,0:T(8,128)(2,1)}), bf16[128,8,1024]{2,1,0:T(8,128)(2,1)S(1)}, u32[]{:S(2)}, u32[]{:S(2)}) %all-to-all-start.1) | async-done | bytes 2097184 | tf_op jit(solution)/shard_map/all_to_all | solution.py:59
  239.8 1.3 copy.29
  (17 shorter events, 0.2 us)
Async XLA Ops:
  7.2 2.8 %copy-start.2 = (s32[1,4]{1,0:T(1,128)S(1)}, s32[1,4]{1,0:T(1,128)}, u32[]{:S(2)}) copy-start(s32[1,4]{1,0:T(1,128)} %param.5) | copy-start | bytes 52
  11.5 11.0 %copy-start.1 = (s32[512,2]{0,1:T(2,128)S(1)}, s32[512,2]{0,1:T(2,128)}, u32[]{:S(2)}) copy-start(s32[512,2]{0,1:T(2,128)} %param.6) | copy-start | bytes 12292
  11.5 43.5 %all-to-all-start = ((bf16[4,512,512]{1,2,0:T(8,128)(2,1)}), bf16[4,512,512]{1,2,0:T(8,128)(2,1)S(1)}, u32[]{:S(2)}, u32[]{:S(2)}) async-start(bf16[4,512,512]{1,2,0:T(8,128)(2,1)} %bitcast_select_fusion.1), calls=%async_computation | async-start | bytes 4194304 | tf_op jit(solution)/shard_map/all_to_all | solution.py:20
  22.5 143.4 %reduce-scatter.2.cloned.1.call-start = ((), (), s32[]{:S(2)}) async-start(), calls=%async_computation.4 | async-start | bytes 5242880 | tf_op jit(solution)/shard_map/reduce_scatter | solution.py:24
  61.6 0.7 copy-start
  66.2 110.9 %all-to-all-start.2 = ((s32[128,1,8]{2,1,0:T(1,128)}), s32[128,1,8]{2,1,0:T(1,128)S(1)}, u32[]{:S(2)}, u32[]{:S(2)}) async-start(s32[128,1,8]{2,1,0:T(1,128)} %bitcast.17), calls=%async_computation.3 | async-start | bytes 131072 | tf_op jit(solution)/shard_map/all_to_all | solution.py:66
  177.1 62.7 %all-to-all-start.1 = ((bf16[128,8,1024]{2,1,0:T(8,128)(2,1)}), bf16[128,8,1024]{2,1,0:T(8,128)(2,1)S(1)}, u32[]{:S(2)}, u32[]{:S(2)}) async-start(bf16[128,8,1024]{2,1,0:T(8,128)(2,1)} %fusion.7), calls=%async_computation.2 | async-start | bytes 4194304 | tf_op jit(solution)/shard_map/all_to_all | solution.py:59
Sparse Core Ops, SparseCore 0:
  61.8 104.0 reduce-scatter.1
where the time goes:
time: 249 us; the launch traced here: 248 us
  waiting for transfers between devices  139 us (56%)
  starting transfers between devices  53.2 us (21%)
  local copies, waits for them, and re-layouts  29.1 us (12%)
  between operations  14.2 us (6%)
  matrix products  6.58 us (3%)
  other arithmetic  5.54 us (2%)
    reduce_scatter x1, waiting for transfers between devices, shards(): lax.psum_scatter(jnp.einsum('jmik,jke->jemi', left_blocks, right_tiles, p...  69.1 us
    all_to_all x1, waiting for transfers between devices, shards(): lax.all_to_all(picked.reshape(clusters, capacity, -1), ('col', 'section')...  50.2 us
    all_to_all x1, starting transfers between devices, shards(): lax.all_to_all(column_ids.reshape(clusters, capacity), ('col', 'section')...  30.4 us
    all_to_all x1, waiting for transfers between devices, shards(): lax.all_to_all(own_column, 'row', split_axis=0, concat_axis=0, tiled=True)  20 us
    all_to_all x1, starting transfers between devices, shards(): lax.all_to_all(picked.reshape(clusters, capacity, -1), ('col', 'section')...  11.9 us
    gather x2, local copies, waits for them, and re-layouts, shards(): jnp.take(own_column, kept_local.reshape(-1), axis=0)  11.6 us
    all_to_all x1, starting transfers between devices, shards(): lax.all_to_all(own_column, 'row', split_axis=0, concat_axis=0, tiled=True)  11 us
    dot_general x1, matrix products, shards(): jnp.einsum('jmik,jke->jemi', left_blocks, right_tiles, preferred_element_...  6.58 us
  transfers between devices with their start and end apart: 4, of which 3 were waited for; matrix products, arithmetic and copies ran while one was open for 11% of the time, Pallas kernels for 0%

commit v1 on v0

v1 whole, which is shorter than its diff:
```python
import jax
import jax.numpy as jnp
from jax import lax
from jax.experimental import pallas as pl
from jax.experimental.pallas import tpu as pltpu
from jax.sharding import PartitionSpec as P

EPS = 1e-6
OWNERS = ("col", "section")


def finish_kernel(first_ref, second_ref, out_ref):
    half = first_ref.shape[-1]
    first = first_ref[...].astype(jnp.float32)
    second = second_ref[...].astype(jnp.float32)
    first = first * first
    second = second * second
    total = jnp.sum(first, axis=-1, keepdims=True) + jnp.sum(second, axis=-1, keepdims=True)
    mean = total * (1.0 / (2 * half)) + EPS
    out_ref[:, :half] = (first / mean).astype(out_ref.dtype)
    out_ref[:, half:] = (second / mean).astype(out_ref.dtype)


def finish(first, second):
    rows, half = first.shape
    step = min(rows, 128)
    spec = pl.BlockSpec((step, half), lambda i: (i, 0))
    return pl.pallas_call(
        finish_kernel,
        grid=(rows // step,),
        in_specs=[spec, spec],
        out_specs=pl.BlockSpec((step, 2 * half), lambda i: (i, 0)),
        out_shape=jax.ShapeDtypeStruct((rows, 2 * half), jnp.bfloat16),
        cost_estimate=pl.CostEstimate(
            flops=6 * rows * half, bytes_accessed=8 * rows * half, transcendentals=0
        ),
        name="finish",
    )(first, second)


def shards(block_vals, present, kept_rows, column_owner):
    size = block_vals.shape[-1]
    places = block_vals.shape[1]
    kept_count = kept_rows.shape[1]
    place = lax.axis_index("row")
    cluster = lax.axis_index("col") * lax.axis_size("section") + lax.axis_index("section")
    clusters = lax.axis_size("col") * lax.axis_size("section")
    capacity = size // lax.axis_size("col")
    slots = clusters * capacity

    def effective(at):
        block = lax.dynamic_index_in_dim(block_vals[0], at, 0, keepdims=False)
        live = jnp.logical_or(
            lax.dynamic_index_in_dim(present[0], at, 0, keepdims=False) > 0, at == place
        )
        return jnp.where(live, block, jnp.zeros_like(block))

    def kept(at, m):
        return kept_rows[at * clusters + cluster, m]

    def outgoing(m):
        return [effective(kept((place + d) % places, m)) for d in range(places)]

    def exchange(blocks):
        return [
            blocks[d]
            if d == 0
            else lax.ppermute(blocks[d], "row", [(i, (i + d) % places) for i in range(places)])
            for d in range(places)
        ]

    left_first = exchange(outgoing(0))

    owners = column_owner[:, 0]
    hits = owners[:, None] == jnp.arange(clusters, dtype=jnp.int32)[None, :]
    index = jnp.arange(size, dtype=jnp.int32)
    before = (index[:, None] > index[None, :]).astype(jnp.bfloat16)
    earlier = jnp.dot(before, hits.astype(jnp.bfloat16), preferred_element_type=jnp.float32)
    order = jnp.sum(jnp.where(hits, earlier, 0.0), axis=1).astype(jnp.int32)
    slot_of = owners * capacity + order
    chosen = jnp.arange(slots, dtype=jnp.int32)[:, None] == slot_of[None, :]
    source = jnp.max(jnp.where(chosen, index[None, :], -1), axis=1)
    ids = jnp.where(source >= 0, (place * clusters + cluster) * size + source, -1)
    arrived_ids = lax.all_to_all(
        ids.reshape(clusters, capacity), OWNERS, split_axis=0, concat_axis=0, tiled=True
    )

    pick = chosen.astype(jnp.bfloat16)
    right = [
        lax.dot_general(
            pick,
            effective((place - d) % places),
            (((1,), (1,)), ((), ())),
            preferred_element_type=jnp.float32,
        ).astype(jnp.bfloat16)
        for d in range(places)
    ]

    def products(left):
        total = None
        for a, b in zip(right, left):
            term = lax.dot_general(
                a, b, (((1,), (1,)), ((), ())), preferred_element_type=jnp.float32
            )
            total = term if total is None else total + term
        return total.astype(jnp.bfloat16)

    def to_owners(values):
        return lax.all_to_all(
            values.reshape(clusters, capacity, size), OWNERS, split_axis=0, concat_axis=0, tiled=True
        ).reshape(slots, size)

    second_out, left_first = lax.optimization_barrier((outgoing(1), left_first))
    left_second = exchange(second_out)
    first_sent = products(left_first)
    first = to_owners(first_sent)
    left_second, first = lax.optimization_barrier((left_second, first))
    second = to_owners(products(left_second))
    pruned = finish(first, second)
    return (
        pruned.reshape(1, 1, clusters, capacity, kept_count * size),
        arrived_ids.reshape(1, 1, clusters, capacity),
    )


def solution(mesh):
    placed = (
        P(("row", "col", "section"), None, None, None),
        P(("row", "col", "section"), None),
        P(),
        P(("row", "col", "section"), None),
    )
    return jax.shard_map(
        shards,
        mesh=mesh,
        in_specs=placed,
        out_specs=(
            P("row", ("col", "section"), None, None, None),
            P("row", ("col", "section"), None, None),
        ),
        check_vma=False,
    )
```

time: 249 us -> 235 us (0.944)
  waiting for transfers between devices: 139 us -> 102 us
  local copies, waits for them, and re-layouts: 29.1 us -> 6.17 us
  between operations: 14.2 us -> 28.9 us
  starting transfers between devices: 53.2 us -> 66.6 us
  matrix products: 6.58 us -> 18.5 us
  Pallas kernels: 0 us -> 6.23 us
    reduce_scatter x1 -> x0, waiting for transfers between devices: 69.1 us -> none  [shards(): lax.psum_scatter(jnp.einsum('jmik,jke->jemi', left_blocks, right_tiles, p...]
    ppermute x0 -> x6, waiting for transfers between devices: none -> 54.5 us  [exchange(): lax.ppermute(blocks[d], 'row', [(i, (i + d) % places) for i in range(plac...]
    ppermute x0 -> x6, starting transfers between devices: none -> 31.5 us  [exchange(): lax.ppermute(blocks[d], 'row', [(i, (i + d) % places) for i in range(plac...]
    all_to_all x3, waiting for transfers between devices: 70.2 us -> 47.9 us  [the longest x2 43.6 us: to_owners(): lax.all_to_all(values.reshape(clusters, capacity, size), OWNERS, split_ax...]
    all_to_all x3, starting transfers between devices: 53.2 us -> 35.1 us  [the longest x2 26.9 us: to_owners(): lax.all_to_all(values.reshape(clusters, capacity, size), OWNERS, split_ax...]
    gather x4 -> x0, local copies, waits for them, and re-layouts: 16.2 us -> none  [the longest x2 11.6 us: shards(): jnp.take(own_column, kept_local.reshape(-1), axis=0)]
    dot_general x1 -> x13, matrix products: 6.58 us -> 18.5 us  [the longest x8 14.2 us: products(): lax.dot_general(a, b, (((1,), (1,)), ((), ())), preferred_element_type=jn...]
    pallas_call x0 -> x1, Pallas kernels: none -> 6.23 us  [finish(): pl.pallas_call(finish_kernel, grid=(rows // step,), in_specs=[spec, spec]...]
  transfers between devices with their start and end apart: 4 -> 9, of which waited for: 3 -> 7; matrix products, arithmetic and copies ran while one was open for 11% -> 6% of each run, Pallas kernels for 0% -> 0%
where the time goes in v1:
time: 235 us; the launch traced here: 234 us
  waiting for transfers between devices  102 us (43%)
  starting transfers between devices  66.6 us (28%)
  between operations  28.9 us (12%)
  matrix products  18.5 us (8%)
  Pallas kernels  6.23 us (3%)
  local copies, waits for them, and re-layouts  6.17 us (3%)
  other arithmetic  4.79 us (2%)
    ppermute x6, waiting for transfers between devices, exchange(): lax.ppermute(blocks[d], 'row', [(i, (i + d) % places) for i in range(plac...  54.5 us
    all_to_all x2, waiting for transfers between devices, to_owners(): lax.all_to_all(values.reshape(clusters, capacity, size), OWNERS, split_ax...  43.6 us
    ppermute x6, starting transfers between devices, exchange(): lax.ppermute(blocks[d], 'row', [(i, (i + d) % places) for i in range(plac...  31.5 us
    all_to_all x2, starting transfers between devices, to_owners(): lax.all_to_all(values.reshape(clusters, capacity, size), OWNERS, split_ax...  26.9 us
    dot_general x8, matrix products, products(): lax.dot_general(a, b, (((1,), (1,)), ((), ())), preferred_element_type=jn...  14.2 us
    all_to_all x1, starting transfers between devices, shards(): lax.all_to_all(ids.reshape(clusters, capacity), OWNERS, split_axis=0, con...  8.22 us
    pallas_call x1, Pallas kernels, finish(): pl.pallas_call(finish_kernel, grid=(rows // step,), in_specs=[spec, spec]...  6.23 us
  transfers between devices with their start and end apart: 9, of which 7 were waited for; matrix products, arithmetic and copies ran while one was open for 6% of the time, Pallas kernels for 0%

profile of v1, /device:TPU:1, one launch (start us, length us, event | category | flops | bytes accessed | tf_op | source)
XLA Modules:
  0.0 233.5 jit_solution(15763791109539356208)
XLA Ops:
  0.7 1.5 constant_dynamic-slice_fusion.5
  22.4 1.8 constant_dynamic-slice_fusion.2
  29.3 0.0 copy-start.10
  29.3 0.0 copy-start
  29.4 4.4 %select_bitcast_fusion = (bf16[512,512]{1,0:T(8,128)(2,1)}, bf16[512,512]{1,0:T(8,128)(2,1)}, bf16[512,512]{1,0:T(8,128)(2,1)}, bf16[512,512]{1,0:T(8,128)(2,1)}...) fusion(bf16[1,4,512,512]{3,2,1,0:T(8,128)(2,1)} %param.4, ...), kind=kLoop, calls=%fused_computation.33 | loop fusion | flops 2097152 | bytes 8388648 | tf_op jit(solution)/shard_map/jit(_where)/select_n | solution.py:56
  33.8 6.6 %collective-permute-start = (bf16[512,512]{1,0:T(8,128)(2,1)}, bf16[512,512]{1,0:T(8,128)(2,1)}, u32[]{:S(2)}, u32[]{:S(2)}) collective-permute-start(bf16[512,512]{1,0:T(8,128)(2,1)} %get-tuple-element.36), channel_id=1, source_target_pairs={{0,128},{128,256},{256,384},{384,0},{1,129},{129,257},{257,385},{3... | collective-permute-start | bytes 1572872 | tf_op jit(solution)/shard_map/ppermute | solution.py:68
  40.4 8.9 %collective-permute-start.1 = (bf16[512,512]{1,0:T(8,128)(2,1)}, bf16[512,512]{1,0:T(8,128)(2,1)}, u32[]{:S(2)}, u32[]{:S(2)}) collective-permute-start(bf16[512,512]{1,0:T(8,128)(2,1)} %get-tuple-element.35), channel_id=1, source_target_pairs={{0,256},{128,384},{256,0},{384,128},{1,257},{129,385},{257,1},{385... | collective-permute-start | bytes 1572872 | tf_op jit(solution)/shard_map/ppermute | solution.py:68
  49.3 3.3 %collective-permute-start.2 = (bf16[512,512]{1,0:T(8,128)(2,1)}, bf16[512,512]{1,0:T(8,128)(2,1)}, u32[]{:S(2)}, u32[]{:S(2)}) collective-permute-start(bf16[512,512]{1,0:T(8,128)(2,1)} %get-tuple-element.34), channel_id=1, source_target_pairs={{0,384},{128,0},{256,128},{384,256},{1,385},{129,1},{257,129},{385... | collective-permute-start | bytes 1572872 | tf_op jit(solution)/shard_map/ppermute | solution.py:68
  52.7 0.0 copy-done.10
  52.7 0.3 fusion.8
  54.3 0.0 copy-done
  54.3 0.8 fusion.6
  55.1 1.7 fusion.4
  58.0 0.8 fusion.5
  58.8 0.0 copy-start.2
  58.8 0.8 fusion.7
  59.5 0.0 copy-start.4
  59.5 0.0 copy-start.1
  59.6 0.0 collective-permute-done
  59.6 11.0 %collective-permute-done.1 = bf16[512,512]{1,0:T(8,128)(2,1)} collective-permute-done((bf16[512,512]{1,0:T(8,128)(2,1)}, bf16[512,512]{1,0:T(8,128)(2,1)}, u32[]{:S(2)}, u32[]{:S(2)}) %collective-permute-start.1) | collective-permute-done | bytes 524320 | tf_op jit(solution)/shard_map/ppermute | solution.py:68
  70.6 26.2 %collective-permute-done.2 = bf16[512,512]{1,0:T(8,128)(2,1)} collective-permute-done((bf16[512,512]{1,0:T(8,128)(2,1)}, bf16[512,512]{1,0:T(8,128)(2,1)}, u32[]{:S(2)}, u32[]{:S(2)}) %collective-permute-start.2) | collective-permute-done | bytes 524320 | tf_op jit(solution)/shard_map/ppermute | solution.py:68
  96.8 1.8 fusion.46
  98.6 0.7 fusion.44
  99.4 1.8 fusion.45
  101.2 2.8 %fusion.9 = bf16[128,8,512]{2,1,0:T(8,128)(2,1)} fusion(f32[1024,512]{1,0:T(8,128)S(1)} %fusion.46, f32[1024,512]{1,0:T(8,128)S(1)} %fusion.44, f32[1024,512]{1,0:T(8,128)S(1)} %fusion.45, bf16[1024,512]{1,0:T(8,128)(2,1)S(1)} %fusion.7, bf16[512,512]{1,0:T(8,128)(2,1)} %collective-permute-done.2), kind=kOutput, calls=%fused_computation.14 | convolution fusion | flops 538968064 | bytes 8912896 | tf_op jit(solution)/shard_map/dot_general | solution.py:102
  103.9 11.5 %all-to-all-start = ((bf16[128,8,512]{2,1,0:T(8,128)(2,1)}), bf16[128,8,512]{2,1,0:T(8,128)(2,1)S(1)}, u32[]{:S(2)}, u32[]{:S(2)}) async-start(bf16[128,8,512]{2,1,0:T(8,128)(2,1)} %fusion.9), calls=%async_computation | async-start | bytes 2097152 | tf_op jit(solution)/shard_map/all_to_all | solution.py:109
  115.5 1.9 collective-permute-start.3
  117.4 7.4 %collective-permute-start.4 = (bf16[512,512]{1,0:T(8,128)(2,1)}, bf16[512,512]{1,0:T(8,128)(2,1)}, u32[]{:S(2)}, u32[]{:S(2)}) collective-permute-start(bf16[512,512]{1,0:T(8,128)(2,1)} %get-tuple-element.17), channel_id=1, source_target_pairs={{0,256},{128,384},{256,0},{384,128},{1,257},{129,385},{257,1},{385... | collective-permute-start | bytes 1572872 | tf_op jit(solution)/shard_map/ppermute | solution.py:68
  124.8 3.3 %collective-permute-start.5 = (bf16[512,512]{1,0:T(8,128)(2,1)}, bf16[512,512]{1,0:T(8,128)(2,1)}, u32[]{:S(2)}, u32[]{:S(2)}) collective-permute-start(bf16[512,512]{1,0:T(8,128)(2,1)} %get-tuple-element.18), channel_id=1, source_target_pairs={{0,384},{128,0},{256,128},{384,256},{1,385},{129,1},{257,129},{385... | collective-permute-start | bytes 1572872 | tf_op jit(solution)/shard_map/ppermute | solution.py:68
  128.1 0.4 select_reduce_fusion
  128.5 0.7 select_n.302
  129.2 15.4 %all-to-all-done = bf16[128,8,512]{2,1,0:T(8,128)(2,1)S(1)} async-done(((bf16[128,8,512]{2,1,0:T(8,128)(2,1)}), bf16[128,8,512]{2,1,0:T(8,128)(2,1)S(1)}, u32[]{:S(2)}, u32[]{:S(2)}) %all-to-all-start) | async-done | bytes 1048608 | tf_op jit(solution)/shard_map/all_to_all | solution.py:109
  144.7 8.2 %all-to-all-start.2 = ((s32[128,1,8]{2,1,0:T(1,128)}), s32[128,1,8]{2,1,0:T(1,128)S(1)}, u32[]{:S(2)}, u32[]{:S(2)}) async-start(s32[128,1,8]{2,1,0:T(1,128)} %bitcast.38), calls=%async_computation.2 | async-start | bytes 131072 | tf_op jit(solution)/shard_map/all_to_all | solution.py:84
  152.9 0.0 copy-start.8
  152.9 0.6 collective-permute-done.3
  153.5 16.7 %collective-permute-done.4 = bf16[512,512]{1,0:T(8,128)(2,1)} collective-permute-done((bf16[512,512]{1,0:T(8,128)(2,1)}, bf16[512,512]{1,0:T(8,128)(2,1)}, u32[]{:S(2)}, u32[]{:S(2)}) %collective-permute-start.4) | collective-permute-done | bytes 524320 | tf_op jit(solution)/shard_map/ppermute | solution.py:68
  170.2 0.0 collective-permute-done.5
  170.2 1.8 fusion.49
  172.0 0.7 fusion.47
  172.7 0.5 copy-done.3
  173.2 1.9 fusion.48
  175.1 2.8 %fusion.10 = bf16[128,8,512]{2,1,0:T(8,128)(2,1)} fusion(f32[1024,512]{1,0:T(8,128)S(1)} %fusion.49, f32[1024,512]{1,0:T(8,128)S(1)} %fusion.47, f32[1024,512]{1,0:T(8,128)S(1)} %fusion.48, bf16[1024,512]{1,0:T(8,128)(2,1)S(1)} %copy-done.5, bf16[512,512]{1,0:T(8,128)(2,1)} %collective-permute-done.5), kind=kOutput, calls=%fused_computation.15 | convolution fusion | flops 538968064 | bytes 8912896 | tf_op jit(solution)/shard_map/dot_general | solution.py:102
  177.8 4.4 %all-to-all-done.2 = s32[128,1,8]{2,1,0:T(1,128)S(1)} async-done(((s32[128,1,8]{2,1,0:T(1,128)}), s32[128,1,8]{2,1,0:T(1,128)S(1)}, u32[]{:S(2)}, u32[]{:S(2)}) %all-to-all-start.2) | async-done | bytes 4128 | tf_op jit(solution)/shard_map/all_to_all | solution.py:84
  182.2 15.3 %all-to-all-start.1 = ((bf16[128,8,512]{2,1,0:T(8,128)(2,1)}), bf16[128,8,512]{2,1,0:T(8,128)(2,1)S(1)}, u32[]{:S(2)}, u32[]{:S(2)}) async-start(bf16[128,8,512]{2,1,0:T(8,128)(2,1)} %fusion.10), calls=%async_computation.1 | async-start | bytes 2097152 | tf_op jit(solution)/shard_map/all_to_all | solution.py:109
  197.5 0.7 copy.10
  198.2 28.1 %all-to-all-done.1 = bf16[128,8,512]{2,1,0:T(8,128)(2,1)S(1)} async-done(((bf16[128,8,512]{2,1,0:T(8,128)(2,1)}), bf16[128,8,512]{2,1,0:T(8,128)(2,1)S(1)}, u32[]{:S(2)}, u32[]{:S(2)}) %all-to-all-start.1) | async-done | bytes 1048608 | tf_op jit(solution)/shard_map/all_to_all | solution.py:109
  226.3 1.0 copy-done.7
  227.3 6.2 %finish.1 = bf16[1024,1024]{1,0:T(8,128)(2,1)} custom-call(bf16[1024,512]{1,0:T(8,128)(2,1)} %bitcast.74, bf16[1024,512]{1,0:T(8,128)(2,1)} %bitcast.75), custom_call_target="tpu_custom_call" | custom-call | flops 3145728 | bytes 4194304 | tf_op jit(solution)/shard_map/finish/pallas_call | solution.py:28
  (14 shorter events, 0.0 us)
Async XLA Ops:
  29.3 23.3 %copy-start.10 = (s32[512,1]{0,1:T(1,128)S(1)}, s32[512,1]{0,1:T(1,128)}, u32[]{:S(2)}) copy-start(s32[512,1]{0,1:T(1,128)} %param.7) | copy-start | bytes 6148
  29.3 24.9 %copy-start = (bf16[1,4,512,512]{3,2,1,0:T(8,128)(2,1)S(1)}, bf16[1,4,512,512]{3,2,1,0:T(8,128)(2,1)}, u32[]{:S(2)}) copy-start(bf16[1,4,512,512]{3,2,1,0:T(8,128)(2,1)} %param.4) | copy-start | bytes 6291460
  33.8 25.8 %collective-permute-start = (bf16[512,512]{1,0:T(8,128)(2,1)}, bf16[512,512]{1,0:T(8,128)(2,1)}, u32[]{:S(2)}, u32[]{:S(2)}) collective-permute-start(bf16[512,512]{1,0:T(8,128)(2,1)} %get-tuple-element.36), channel_id=1, source_target_pairs={{0,128},{128,256},{256,384},{384,0},{1,129},{129,257},{257,385},{3... | collective-permute-start | bytes 1572872 | tf_op jit(solution)/shard_map/ppermute | solution.py:68
  40.4 30.2 %collective-permute-start.1 = (bf16[512,512]{1,0:T(8,128)(2,1)}, bf16[512,512]{1,0:T(8,128)(2,1)}, u32[]{:S(2)}, u32[]{:S(2)}) collective-permute-start(bf16[512,512]{1,0:T(8,128)(2,1)} %get-tuple-element.35), channel_id=1, source_target_pairs={{0,256},{128,384},{256,0},{384,128},{1,257},{129,385},{257,1},{385... | collective-permute-start | bytes 1572872 | tf_op jit(solution)/shard_map/ppermute | solution.py:68
  49.3 47.5 %collective-permute-start.2 = (bf16[512,512]{1,0:T(8,128)(2,1)}, bf16[512,512]{1,0:T(8,128)(2,1)}, u32[]{:S(2)}, u32[]{:S(2)}) collective-permute-start(bf16[512,512]{1,0:T(8,128)(2,1)} %get-tuple-element.34), channel_id=1, source_target_pairs={{0,384},{128,0},{256,128},{384,256},{1,385},{129,1},{257,129},{385... | collective-permute-start | bytes 1572872 | tf_op jit(solution)/shard_map/ppermute | solution.py:68
  58.8 40.6 %copy-start.2 = (bf16[1024,512]{1,0:T(8,128)(2,1)}, bf16[1024,512]{1,0:T(8,128)(2,1)S(1)}, u32[]{:S(2)}) copy-start(bf16[1024,512]{1,0:T(8,128)(2,1)S(1)} %fusion.5) | copy-start | bytes 3145732
  59.5 41.6 %copy-start.4 = (bf16[1024,512]{1,0:T(8,128)(2,1)}, bf16[1024,512]{1,0:T(8,128)(2,1)S(1)}, u32[]{:S(2)}) copy-start(bf16[1024,512]{1,0:T(8,128)(2,1)S(1)} %fusion.7) | copy-start | bytes 3145732
  59.5 39.1 %copy-start.1 = (bf16[1024,512]{1,0:T(8,128)(2,1)S(1)}, bf16[1024,512]{1,0:T(8,128)(2,1)}, u32[]{:S(2)}) copy-start(bf16[1024,512]{1,0:T(8,128)(2,1)} %fusion.4) | copy-start | bytes 3145732
  59.6 39.1 %copy-start.9 = (bf16[512,512]{1,0:T(8,128)(2,1)S(1)}, bf16[512,512]{1,0:T(8,128)(2,1)}, u32[]{:S(2)}) copy-start(bf16[512,512]{1,0:T(8,128)(2,1)} %get-tuple-element.19) | copy-start | bytes 1572868
  103.9 40.7 %all-to-all-start = ((bf16[128,8,512]{2,1,0:T(8,128)(2,1)}), bf16[128,8,512]{2,1,0:T(8,128)(2,1)S(1)}, u32[]{:S(2)}, u32[]{:S(2)}) async-start(bf16[128,8,512]{2,1,0:T(8,128)(2,1)} %fusion.9), calls=%async_computation | async-start | bytes 2097152 | tf_op jit(solution)/shard_map/all_to_all | solution.py:109
  115.5 38.0 %collective-permute-start.3 = (bf16[512,512]{1,0:T(8,128)(2,1)}, bf16[512,512]{1,0:T(8,128)(2,1)}, u32[]{:S(2)}, u32[]{:S(2)}) collective-permute-start(bf16[512,512]{1,0:T(8,128)(2,1)} %get-tuple-element.16), channel_id=1, source_target_pairs={{0,128},{128,256},{256,384},{384,0},{1,129},{129,257},{257,385},{3... | collective-permute-start | bytes 1572872 | tf_op jit(solution)/shard_map/ppermute | solution.py:68
  117.4 52.7 %collective-permute-start.4 = (bf16[512,512]{1,0:T(8,128)(2,1)}, bf16[512,512]{1,0:T(8,128)(2,1)}, u32[]{:S(2)}, u32[]{:S(2)}) collective-permute-start(bf16[512,512]{1,0:T(8,128)(2,1)} %get-tuple-element.17), channel_id=1, source_target_pairs={{0,256},{128,384},{256,0},{384,128},{1,257},{129,385},{257,1},{385... | collective-permute-start | bytes 1572872 | tf_op jit(solution)/shard_map/ppermute | solution.py:68
  124.8 45.4 %collective-permute-start.5 = (bf16[512,512]{1,0:T(8,128)(2,1)}, bf16[512,512]{1,0:T(8,128)(2,1)}, u32[]{:S(2)}, u32[]{:S(2)}) collective-permute-start(bf16[512,512]{1,0:T(8,128)(2,1)} %get-tuple-element.18), channel_id=1, source_target_pairs={{0,384},{128,0},{256,128},{384,256},{1,385},{129,1},{257,129},{385... | collective-permute-start | bytes 1572872 | tf_op jit(solution)/shard_map/ppermute | solution.py:68
  144.6 28.1 %copy-start.6 = (bf16[128,8,512]{2,1,0:T(8,128)(2,1)}, bf16[128,8,512]{2,1,0:T(8,128)(2,1)S(1)}, u32[]{:S(2)}) copy-start(bf16[128,8,512]{2,1,0:T(8,128)(2,1)S(1)} %all-to-all-done) | copy-start | bytes 3145732
  144.7 37.5 %all-to-all-start.2 = ((s32[128,1,8]{2,1,0:T(1,128)}), s32[128,1,8]{2,1,0:T(1,128)S(1)}, u32[]{:S(2)}, u32[]{:S(2)}) async-start(s32[128,1,8]{2,1,0:T(1,128)} %bitcast.38), calls=%async_computation.2 | async-start | bytes 131072 | tf_op jit(solution)/shard_map/all_to_all | solution.py:84
  152.9 19.1 %copy-start.8 = (bf16[512,512]{1,0:T(8,128)(2,1)S(1)}, bf16[512,512]{1,0:T(8,128)(2,1)}, u32[]{:S(2)}) copy-start(bf16[512,512]{1,0:T(8,128)(2,1)} %get-tuple-element.24) | copy-start | bytes 1572868
  172.0 1.2 copy-start.3
  173.2 1.9 copy-start.5
  182.2 44.1 %all-to-all-start.1 = ((bf16[128,8,512]{2,1,0:T(8,128)(2,1)}), bf16[128,8,512]{2,1,0:T(8,128)(2,1)S(1)}, u32[]{:S(2)}, u32[]{:S(2)}) async-start(bf16[128,8,512]{2,1,0:T(8,128)(2,1)} %fusion.10), calls=%async_computation.1 | async-start | bytes 2097152 | tf_op jit(solution)/shard_map/all_to_all | solution.py:109
  226.3 1.0 copy-start.7

commit v2 on v1

v2 whole, which is shorter than its diff:
```python
import jax
import jax.numpy as jnp
from jax import lax
from jax.experimental import pallas as pl
from jax.experimental.pallas import tpu as pltpu
from jax.sharding import PartitionSpec as P

EPS = 1e-6
OWNERS = ("col", "section")
TILES = 4
CHUNKS = (((0, 0, 8),), ((1, 0, 8),))


def segments(chunk, size):
    out, at = [], 0
    for m, first, last in chunk:
        rows = (last - first) * size // 8
        out.append((m, first * size // 8, at, rows))
        at += rows
    return out, at


def own_cluster():
    return lax.axis_index("col") * lax.axis_size("section") + lax.axis_index("section")


def needed(m, target, present_ref, kept_ref):
    clusters = lax.axis_size("col") * lax.axis_size("section")
    block = target if m == 0 else kept_ref[m, target * clusters + own_cluster()]
    live = jnp.logical_or(present_ref[0, block] > 0, block == lax.axis_index("row"))
    return block, live


def stage_kernel(chunk, present_ref, kept_ref, blocks_ref, *refs):
    places, size = present_ref.shape[1], blocks_ref.shape[-1]
    outs, (held, in_sems, out_sems) = refs[:-3], refs[-3:]
    place = lax.axis_index("row")
    parts = segments(chunk, size)[0]
    loads = []
    for k in range(places - 1):
        target = lax.rem(place + k + 1, places)
        for i, (m, first, at, rows) in enumerate(parts):
            block, live = needed(m, target, present_ref, kept_ref)
            load = pltpu.make_async_copy(
                blocks_ref.at[0, block, pl.ds(first, rows)],
                held.at[k, pl.ds(at, rows)],
                in_sems.at[k, i],
            )
            loads.append((k, live, load))

            @pl.when(live)
            def _():
                load.start()

            @pl.when(jnp.logical_not(live))
            def _():
                held[k, at : at + rows, :] = jnp.zeros((rows, size), held.dtype)

    stores = [
        pltpu.make_async_copy(held.at[k], outs[k], out_sems.at[k]) for k in range(places - 1)
    ]
    for i, (k, live, load) in enumerate(loads):

        @pl.when(live)
        def _():
            load.wait()

        if i % len(parts) == len(parts) - 1:
            stores[k].start()
    for store in stores:
        store.wait()


def stage(chunk, block_vals, present, kept_rows):
    others, size = block_vals.shape[1] - 1, block_vals.shape[-1]
    rows = segments(chunk, size)[1]
    return pl.pallas_call(
        lambda *refs: stage_kernel(chunk, *refs),
        in_specs=[
            pl.BlockSpec(memory_space=pltpu.SMEM),
            pl.BlockSpec(memory_space=pltpu.SMEM),
            pl.BlockSpec(memory_space=pl.ANY),
        ],
        out_specs=[pl.BlockSpec(memory_space=pl.ANY)] * others,
        out_shape=[jax.ShapeDtypeStruct((rows, size), block_vals.dtype)] * others,
        scratch_shapes=[
            pltpu.VMEM((others, rows, size), block_vals.dtype),
            pltpu.SemaphoreType.DMA((others, len(chunk))),
            pltpu.SemaphoreType.DMA((others,)),
        ],
        cost_estimate=pl.CostEstimate(
            flops=0, bytes_accessed=4 * others * rows * size, transcendentals=0
        ),
        name="stage",
    )(present, kept_rows.T, block_vals)


def products_kernel(chunk, present_ref, kept_ref, slot_ref, blocks_ref, *refs):
    places, size = present_ref.shape[1], slot_ref.shape[1]
    lefts, out_ref = refs[:-1], refs[-1]
    place = lax.axis_index("row")
    own = []
    for m, first, _, rows in segments(chunk, size)[0]:
        block, live = needed(m, place, present_ref, kept_ref)
        part = blocks_ref[0, block, first : first + rows, :]
        own.append(jnp.where(live, part, jnp.zeros_like(part)))
    own = own[0] if len(own) == 1 else jnp.concatenate(own, axis=0)
    total = jnp.dot(own, blocks_ref[0, place], preferred_element_type=jnp.float32)
    for k in range(places - 1):
        at = lax.rem(place + places - 1 - k, places)
        live = present_ref[0, at] > 0
        term = jnp.dot(lefts[k][...], blocks_ref[0, at], preferred_element_type=jnp.float32)
        total = total + jnp.where(live, term, jnp.zeros_like(term))
    expanded = total.astype(jnp.bfloat16)
    slots = out_ref.shape[0]
    step = slots // TILES
    for i in range(TILES):
        here = i * step + lax.broadcasted_iota(jnp.int32, (step, size), 0)
        pick = jnp.where(here == slot_ref[...], 1.0, 0.0).astype(jnp.bfloat16)
        out_ref[i * step : (i + 1) * step, :] = lax.dot_general(
            pick, expanded, (((1,), (1,)), ((), ())), preferred_element_type=jnp.float32
        ).astype(out_ref.dtype)


def products(chunk, present, kept_rows, slot_of, block_vals, left, slots):
    size = block_vals.shape[-1]
    rows = left[0].shape[0]
    smem = pl.BlockSpec(memory_space=pltpu.SMEM)
    vmem = pl.BlockSpec(memory_space=pltpu.VMEM)
    return pl.pallas_call(
        lambda *refs: products_kernel(chunk, *refs),
        in_specs=[smem, smem, vmem, vmem] + [vmem] * len(left),
        out_specs=vmem,
        out_shape=jax.ShapeDtypeStruct((slots, rows), jnp.bfloat16),
        compiler_params=pltpu.CompilerParams(vmem_limit_bytes=32 * 2**20),
        cost_estimate=pl.CostEstimate(
            flops=50_000_000_000, bytes_accessed=8 * size * size, transcendentals=0
        ),
        name="products",
    )(present, kept_rows.T, slot_of.reshape(1, size), block_vals, *left)


def finish_kernel(*refs):
    count = len(CHUNKS)
    arrived, out_ref = refs[:count], refs[count]
    held, result, in_sems, out_sems = refs[count + 1 : 2 * count + 1], *refs[2 * count + 1 :]
    rows, wide = result.shape
    size = wide // 2
    step = rows // TILES
    loads = [
        [
            pltpu.make_async_copy(
                arrived[c].at[pl.ds(i * step, step)],
                held[c].at[pl.ds(i * step, step)],
                in_sems.at[c, i],
            )
            for c in range(count)
        ]
        for i in range(TILES)
    ]
    for tile in loads:
        for load in tile:
            load.start()
    stores = []
    for i in range(TILES):
        part = slice(i * step, (i + 1) * step)
        squares, total = [], 0.0
        for c in range(count):
            loads[i][c].wait()
            value = held[c][part, :].astype(jnp.float32)
            squares.append(value * value)
            total = total + jnp.sum(squares[c], axis=-1, keepdims=True)
        scale = 1.0 / (total * (1.0 / wide) + EPS)
        for c in range(count):
            for m, first, at, length in segments(CHUNKS[c], size)[0]:
                result[part, m * size + first : m * size + first + length] = (
                    squares[c][:, at : at + length] * scale
                ).astype(result.dtype)
        stores.append(
            pltpu.make_async_copy(
                result.at[pl.ds(i * step, step)], out_ref.at[pl.ds(i * step, step)], out_sems.at[i]
            )
        )
        stores[i].start()
    for store in stores:
        store.wait()


def finish(arrived, wide):
    rows = arrived[0].shape[0]
    return pl.pallas_call(
        finish_kernel,
        in_specs=[pl.BlockSpec(memory_space=pl.ANY)] * len(arrived),
        out_specs=pl.BlockSpec(memory_space=pltpu.HBM),
        out_shape=jax.ShapeDtypeStruct((rows, wide), jnp.bfloat16),
        scratch_shapes=[pltpu.VMEM(a.shape, a.dtype) for a in arrived]
        + [
            pltpu.VMEM((rows, wide), jnp.bfloat16),
            pltpu.SemaphoreType.DMA((len(arrived), TILES)),
            pltpu.SemaphoreType.DMA((TILES,)),
        ],
        compiler_params=pltpu.CompilerParams(vmem_limit_bytes=32 * 2**20),
        cost_estimate=pl.CostEstimate(
            flops=3 * rows * wide, bytes_accessed=4 * rows * wide, transcendentals=0
        ),
        name="finish",
    )(*arrived)


def shards(block_vals, present, kept_rows, column_owner):
    size = block_vals.shape[-1]
    places = block_vals.shape[1]
    kept_count = kept_rows.shape[1]
    place = lax.axis_index("row")
    cluster = lax.axis_index("col") * lax.axis_size("section") + lax.axis_index("section")
    clusters = lax.axis_size("col") * lax.axis_size("section")
    capacity = size // lax.axis_size("col")
    slots = clusters * capacity

    def exchange(blocks):
        return [
            lax.ppermute(block, "row", [(i, (i + k + 1) % places) for i in range(places)])
            for k, block in enumerate(blocks)
        ]

    def to_owners(values):
        values = values.reshape(clusters, capacity, -1)
        return lax.all_to_all(values, OWNERS, split_axis=0, concat_axis=0, tiled=True)

    staged = stage(CHUNKS[0], block_vals, present, kept_rows)
    owners, here, staged = lax.optimization_barrier((column_owner[:, 0], present, staged))
    left_first = exchange(staged)

    hits = owners[:, None] == jnp.arange(clusters, dtype=jnp.int32)[None, :]
    index = jnp.arange(size, dtype=jnp.int32)
    before = (index[:, None] > index[None, :]).astype(jnp.bfloat16)
    earlier = jnp.dot(before, hits.astype(jnp.bfloat16), preferred_element_type=jnp.float32)
    order = jnp.sum(jnp.where(hits, earlier, 0.0), axis=1).astype(jnp.int32)
    slot_of = owners * capacity + order
    chosen = jnp.arange(slots, dtype=jnp.int32)[:, None] == slot_of[None, :]
    source = jnp.max(jnp.where(chosen, index[None, :], -1), axis=1)
    ids = jnp.where(source >= 0, (place * clusters + cluster) * size + source, -1)
    ids, here = lax.optimization_barrier((ids, here))
    arrived_ids = lax.all_to_all(
        ids.reshape(clusters, capacity), OWNERS, split_axis=0, concat_axis=0, tiled=True
    )

    left_second = exchange(stage(CHUNKS[1], block_vals, here, kept_rows))
    first = products(CHUNKS[0], present, kept_rows, slot_of, block_vals, left_first, slots)
    slot_later = lax.optimization_barrier((first, slot_of))[1]
    first = to_owners(first)
    second = to_owners(
        products(CHUNKS[1], present, kept_rows, slot_later, block_vals, left_second, slots)
    )
    arrived = [first.reshape(slots, -1), second.reshape(slots, -1)]
    pruned = finish(arrived, kept_count * size)
    return (
        pruned.reshape(1, 1, clusters, capacity, kept_count * size),
        arrived_ids.reshape(1, 1, clusters, capacity),
    )


def solution(mesh):
    placed = (
        P(("row", "col", "section"), None, None, None),
        P(("row", "col", "section"), None),
        P(),
        P(("row", "col", "section"), None),
    )
    return jax.shard_map(
        shards,
        mesh=mesh,
        in_specs=placed,
        out_specs=(
            P("row", ("col", "section"), None, None, None),
            P("row", ("col", "section"), None, None),
        ),
        check_vma=False,
    )
```

time: 235 us -> 170 us (0.72)
  between operations: 28.9 us -> 0.86 us
  waiting for transfers between devices: 102 us -> 79.2 us
  matrix products: 18.5 us -> 0.31 us
  Pallas kernels: 6.23 us -> 15 us
  other arithmetic: 4.79 us -> 0.37 us
  starting transfers between devices: 66.6 us -> 69.8 us
  local copies, waits for them, and re-layouts: 6.17 us -> 3.33 us
    dot_general x12 -> x0, matrix products: 18.2 us -> none  [the longest x8 14.2 us: products(): lax.dot_general(a, b, (((1,), (1,)), ((), ())), preferred_element_type=jn...]
    all_to_all x2, waiting for transfers between devices: 43.6 us -> 30.7 us  [to_owners(): lax.all_to_all(values, OWNERS, split_axis=0, concat_axis=0, tiled=True)]
    pallas_call x1 -> x5, Pallas kernels: 6.23 us -> 15 us  [the longest x2 6.53 us: stage(): pl.pallas_call(lambda *refs: stage_kernel(chunk, *refs), in_specs=[pl.Blo...]
    ppermute x6, waiting for transfers between devices: 54.5 us -> 48.5 us  [exchange(): lax.ppermute(block, 'row', [(i, (i + k + 1) % places) for i in range(plac...]
    all_to_all x1, starting transfers between devices: 8.22 us -> 13.5 us  [shards(): lax.all_to_all(ids.reshape(clusters, capacity), OWNERS, split_axis=0, con...]
    select_n x1 -> x0, other arithmetic: 4.42 us -> none  [effective(): return jnp.where(live, block, jnp.zeros_like(block))]
    all_to_all x1, waiting for transfers between devices: 4.36 us -> 0.01 us  [shards(): lax.all_to_all(ids.reshape(clusters, capacity), OWNERS, split_axis=0, con...]
    dynamic_slice x2 -> x0, local copies, waits for them, and re-layouts: 3.3 us -> none  [the longest x1 1.8 us: effective(): lax.dynamic_index_in_dim(present[0], at, 0, keepdims=False) > 0]
  transfers between devices with their start and end apart: 9 -> 9, of which waited for: 7 -> 4; matrix products, arithmetic and copies ran while one was open for 6% -> 1% of each run, Pallas kernels for 0% -> 6%
where the time goes in v2:
time: 170 us; the launch traced here: 169 us
  waiting for transfers between devices  79.2 us (47%)
  starting transfers between devices  69.8 us (41%)
  Pallas kernels  15 us (9%)
  local copies, waits for them, and re-layouts  3.33 us (2%)
    ppermute x6, waiting for transfers between devices, exchange(): lax.ppermute(block, 'row', [(i, (i + k + 1) % places) for i in range(plac...  48.5 us
    all_to_all x2, waiting for transfers between devices, to_owners(): lax.all_to_all(values, OWNERS, split_axis=0, concat_axis=0, tiled=True)  30.7 us
    ppermute x6, starting transfers between devices, exchange(): lax.ppermute(block, 'row', [(i, (i + k + 1) % places) for i in range(plac...  29.1 us
    all_to_all x2, starting transfers between devices, to_owners(): lax.all_to_all(values, OWNERS, split_axis=0, concat_axis=0, tiled=True)  27.2 us
    all_to_all x1, starting transfers between devices, shards(): lax.all_to_all(ids.reshape(clusters, capacity), OWNERS, split_axis=0, con...  13.5 us
    pallas_call x2, Pallas kernels, stage(): pl.pallas_call(lambda *refs: stage_kernel(chunk, *refs), in_specs=[pl.Blo...  6.53 us
    pallas_call x2, Pallas kernels, products(): pl.pallas_call(lambda *refs: products_kernel(chunk, *refs), in_specs=[sme...  6.32 us
  transfers between devices with their start and end apart: 9, of which 4 were waited for; matrix products, arithmetic and copies ran while one was open for 1% of the time, Pallas kernels for 6%

profile of v2, /device:TPU:1, one launch (start us, length us, event | category | flops | bytes accessed | tf_op | source)
XLA Modules:
  0.0 168.8 jit_solution(12804771474069978116)
XLA Ops:
  0.6 0.0 copy-start.5
  0.6 0.0 copy-start
  0.7 0.0 copy-start.3
  0.7 0.0 copy-start.4
  0.7 3.1 %stage.2 = (bf16[512,512]{1,0:T(8,128)(2,1)}, bf16[512,512]{1,0:T(8,128)(2,1)}, bf16[512,512]{1,0:T(8,128)(2,1)}) custom-call(s32[1,4]{1,0:T(1,128)} %refs_0_.6, s32[2,512]{1,0:T(2,128)} %bitcast.15, bf16[1,4,512,512]{3,2,1,0:T(8,128)(2,1)} %refs_3_.3), custom_call_target="tpu_custom_call" | custom-call | bytes 3145728 | tf_op jit(solution)/shard_map/stage/pallas_call | solution.py:77
  3.8 6.6 %collective-permute-start = (bf16[512,512]{1,0:T(8,128)(2,1)}, bf16[512,512]{1,0:T(8,128)(2,1)S(1)}, u32[]{:S(2)}, u32[]{:S(2)}) collective-permute-start(bf16[512,512]{1,0:T(8,128)(2,1)} %get-tuple-element.20), channel_id=1, source_target_pairs={{0,128},{128,256},{256,384},{384,0},{1,129},{129,257},{257,385},{3... | collective-permute-start | bytes 1572872 | tf_op jit(solution)/shard_map/ppermute | solution.py:222
  10.4 8.8 %collective-permute-start.1 = (bf16[512,512]{1,0:T(8,128)(2,1)}, bf16[512,512]{1,0:T(8,128)(2,1)S(1)}, u32[]{:S(2)}, u32[]{:S(2)}) collective-permute-start(bf16[512,512]{1,0:T(8,128)(2,1)} %get-tuple-element.21), channel_id=1, source_target_pairs={{0,256},{128,384},{256,0},{384,128},{1,257},{129,385},{257,1},{385... | collective-permute-start | bytes 1572872 | tf_op jit(solution)/shard_map/ppermute | solution.py:222
  19.3 3.4 %collective-permute-start.2 = (bf16[512,512]{1,0:T(8,128)(2,1)}, bf16[512,512]{1,0:T(8,128)(2,1)}, u32[]{:S(2)}, u32[]{:S(2)}) collective-permute-start(bf16[512,512]{1,0:T(8,128)(2,1)} %get-tuple-element.22), channel_id=1, source_target_pairs={{0,384},{128,0},{256,128},{384,256},{1,385},{129,1},{257,129},{385... | collective-permute-start | bytes 1572872 | tf_op jit(solution)/shard_map/ppermute | solution.py:222
  22.7 0.0 copy-done.5
  22.7 0.3 fusion
  23.0 0.4 select_reduce_fusion
  23.4 0.7 all_to_all.14
  24.1 13.5 %all-to-all-start.2 = ((s32[128,1,8]{2,1,0:T(1,128)}), s32[128,1,8]{2,1,0:T(1,128)S(1)}, u32[]{:S(2)}, u32[]{:S(2)}) async-start(s32[128,1,8]{2,1,0:T(1,128)} %bitcast.9), calls=%async_computation.2 | async-start | bytes 131072 | tf_op jit(solution)/shard_map/all_to_all | solution.py:244
  37.6 3.4 %stage.3 = (bf16[512,512]{1,0:T(8,128)(2,1)}, bf16[512,512]{1,0:T(8,128)(2,1)}, bf16[512,512]{1,0:T(8,128)(2,1)}) custom-call(s32[1,4]{1,0:T(1,128)} %refs_0_.6, s32[2,512]{1,0:T(2,128)} %bitcast.16, bf16[1,4,512,512]{3,2,1,0:T(8,128)(2,1)} %refs_3_.3), custom_call_target="tpu_custom_call" | custom-call | bytes 3145728 | tf_op jit(solution)/shard_map/stage/pallas_call | solution.py:77
  41.0 2.5 %collective-permute-start.3 = (bf16[512,512]{1,0:T(8,128)(2,1)}, bf16[512,512]{1,0:T(8,128)(2,1)}, u32[]{:S(2)}, u32[]{:S(2)}) collective-permute-start(bf16[512,512]{1,0:T(8,128)(2,1)} %get-tuple-element.26), channel_id=1, source_target_pairs={{0,128},{128,256},{256,384},{384,0},{1,129},{129,257},{257,385},{3... | collective-permute-start | bytes 1572872 | tf_op jit(solution)/shard_map/ppermute | solution.py:222
  43.5 2.7 %collective-permute-start.4 = (bf16[512,512]{1,0:T(8,128)(2,1)}, bf16[512,512]{1,0:T(8,128)(2,1)}, u32[]{:S(2)}, u32[]{:S(2)}) collective-permute-start(bf16[512,512]{1,0:T(8,128)(2,1)} %get-tuple-element.27), channel_id=1, source_target_pairs={{0,256},{128,384},{256,0},{384,128},{1,257},{129,385},{257,1},{385... | collective-permute-start | bytes 1572872 | tf_op jit(solution)/shard_map/ppermute | solution.py:222
  46.2 0.0 collective-permute-done.refs_4_
  46.2 5.1 %collective-permute-start.5 = (bf16[512,512]{1,0:T(8,128)(2,1)}, bf16[512,512]{1,0:T(8,128)(2,1)}, u32[]{:S(2)}, u32[]{:S(2)}) collective-permute-start(bf16[512,512]{1,0:T(8,128)(2,1)} %get-tuple-element.28), channel_id=1, source_target_pairs={{0,384},{128,0},{256,128},{384,256},{1,385},{129,1},{257,129},{385... | collective-permute-start | bytes 1572872 | tf_op jit(solution)/shard_map/ppermute | solution.py:222
  51.3 0.0 collective-permute-done.1.refs_5_
  51.3 21.0 %collective-permute-done.2.refs_6_ = bf16[512,512]{1,0:T(8,128)(2,1)} collective-permute-done((bf16[512,512]{1,0:T(8,128)(2,1)}, bf16[512,512]{1,0:T(8,128)(2,1)}, u32[]{:S(2)}, u32[]{:S(2)}) %collective-permute-start.2) | collective-permute-done | bytes 524320 | tf_op jit(solution)/shard_map/ppermute | solution.py:222
  72.3 0.0 copy-done
  72.3 0.0 copy-done.3
  72.3 0.0 copy-done.4
  72.3 3.0 %products.2 = bf16[1024,512]{1,0:T(8,128)(2,1)S(1)} custom-call(s32[1,4]{1,0:T(1,128)S(1)} %copy-done.4, s32[2,512]{1,0:T(2,128)S(1)} %bitcast.17, s32[1,512]{1,0:T(1,128)S(1)} %bitcast.19, bf16[1,4,512,512]{3,2,1,0:T(8,128)(2,1)S(1)} %copy-done, bf16[512,512]{1,0:T(8,128)(2,1)S(1)} %collective-permute-done.refs_4_, ...), custom_call_target="tpu_custom_call" | custom-call | flops 49999998976 | bytes 2097152 | tf_op jit(solution)/shard_map/products/pallas_call | solution.py:130
  75.3 0.0 copy-start.1
  75.4 1.0 copy-done.1
  76.3 0.0 all-to-all-done.2
  76.3 15.1 %all-to-all-start = ((bf16[128,8,512]{2,1,0:T(8,128)(2,1)}), bf16[128,8,512]{2,1,0:T(8,128)(2,1)S(1)}, u32[]{:S(2)}, u32[]{:S(2)}) async-start(bf16[128,8,512]{2,1,0:T(8,128)(2,1)} %bitcast.13), calls=%async_computation | async-start | bytes 2097152 | tf_op jit(solution)/shard_map/all_to_all | solution.py:228
  91.4 0.0 collective-permute-done.3.refs_4_
  91.5 27.5 %collective-permute-done.4.refs_5_ = bf16[512,512]{1,0:T(8,128)(2,1)} collective-permute-done((bf16[512,512]{1,0:T(8,128)(2,1)}, bf16[512,512]{1,0:T(8,128)(2,1)}, u32[]{:S(2)}, u32[]{:S(2)}) %collective-permute-start.4) | collective-permute-done | bytes 524320 | tf_op jit(solution)/shard_map/ppermute | solution.py:222
  119.0 0.0 collective-permute-done.5.refs_6_
  119.0 3.3 %products.3 = bf16[1024,512]{1,0:T(8,128)(2,1)S(1)} custom-call(s32[1,4]{1,0:T(1,128)S(1)} %copy-done.4, s32[2,512]{1,0:T(2,128)S(1)} %bitcast.18, s32[1,512]{1,0:T(1,128)S(1)} %bitcast.20, bf16[1,4,512,512]{3,2,1,0:T(8,128)(2,1)S(1)} %copy-done, bf16[512,512]{1,0:T(8,128)(2,1)} %collective-permute-done.3.refs_4_, ...), custom_call_target="tpu_custom_call" | custom-call | flops 49999998976 | bytes 2097152 | tf_op jit(solution)/shard_map/products/pallas_call | solution.py:130
  122.3 0.0 copy-start.2
  122.3 1.0 copy-done.2
  123.3 2.5 %all-to-all-done = bf16[128,8,512]{2,1,0:T(8,128)(2,1)S(1)} async-done(((bf16[128,8,512]{2,1,0:T(8,128)(2,1)}), bf16[128,8,512]{2,1,0:T(8,128)(2,1)S(1)}, u32[]{:S(2)}, u32[]{:S(2)}) %all-to-all-start) | async-done | bytes 1048608 | tf_op jit(solution)/shard_map/all_to_all | solution.py:228
  125.8 12.1 %all-to-all-start.1 = ((bf16[128,8,512]{2,1,0:T(8,128)(2,1)}), bf16[128,8,512]{2,1,0:T(8,128)(2,1)S(1)}, u32[]{:S(2)}, u32[]{:S(2)}) async-start(bf16[128,8,512]{2,1,0:T(8,128)(2,1)} %bitcast.14), calls=%async_computation.1 | async-start | bytes 2097152 | tf_op jit(solution)/shard_map/all_to_all | solution.py:228
  137.9 0.7 copy.10
  138.5 28.1 %all-to-all-done.1 = bf16[128,8,512]{2,1,0:T(8,128)(2,1)S(1)} async-done(((bf16[128,8,512]{2,1,0:T(8,128)(2,1)}), bf16[128,8,512]{2,1,0:T(8,128)(2,1)S(1)}, u32[]{:S(2)}, u32[]{:S(2)}) %all-to-all-start.1) | async-done | bytes 1048608 | tf_op jit(solution)/shard_map/all_to_all | solution.py:228
  166.7 2.2 %finish.1 = bf16[1024,1024]{1,0:T(8,128)(2,1)} custom-call(bf16[1024,512]{1,0:T(8,128)(2,1)S(1)} %bitcast.11, bf16[1024,512]{1,0:T(8,128)(2,1)S(1)} %bitcast.12), custom_call_target="tpu_custom_call" | custom-call | flops 3145728 | bytes 4194304 | tf_op jit(solution)/shard_map/finish/pallas_call | solution.py:191
  (2 shorter events, 0.0 us)
Async XLA Ops:
  0.6 22.1 %copy-start.5 = (s32[512,1]{0,1:T(1,128)S(1)}, s32[512,1]{0,1:T(1,128)}, u32[]{:S(2)}) copy-start(s32[512,1]{0,1:T(1,128)} %param.7) | copy-start | bytes 6148
  0.6 71.7 %copy-start = (bf16[1,4,512,512]{3,2,1,0:T(8,128)(2,1)S(1)}, bf16[1,4,512,512]{3,2,1,0:T(8,128)(2,1)}, u32[]{:S(2)}) copy-start(bf16[1,4,512,512]{3,2,1,0:T(8,128)(2,1)} %refs_3_.3) | copy-start | bytes 6291460
  0.7 71.7 %copy-start.3 = (s32[512,2]{0,1:T(2,128)S(1)}, s32[512,2]{0,1:T(2,128)}, u32[]{:S(2)}) copy-start(s32[512,2]{0,1:T(2,128)} %param.6) | copy-start | bytes 12292
  0.7 71.7 %copy-start.4 = (s32[1,4]{1,0:T(1,128)S(1)}, s32[1,4]{1,0:T(1,128)}, u32[]{:S(2)}) copy-start(s32[1,4]{1,0:T(1,128)} %refs_0_.6) | copy-start | bytes 52
  3.8 42.4 %collective-permute-start = (bf16[512,512]{1,0:T(8,128)(2,1)}, bf16[512,512]{1,0:T(8,128)(2,1)S(1)}, u32[]{:S(2)}, u32[]{:S(2)}) collective-permute-start(bf16[512,512]{1,0:T(8,128)(2,1)} %get-tuple-element.20), channel_id=1, source_target_pairs={{0,128},{128,256},{256,384},{384,0},{1,129},{129,257},{257,385},{3... | collective-permute-start | bytes 1572872 | tf_op jit(solution)/shard_map/ppermute | solution.py:222
  10.4 40.9 %collective-permute-start.1 = (bf16[512,512]{1,0:T(8,128)(2,1)}, bf16[512,512]{1,0:T(8,128)(2,1)S(1)}, u32[]{:S(2)}, u32[]{:S(2)}) collective-permute-start(bf16[512,512]{1,0:T(8,128)(2,1)} %get-tuple-element.21), channel_id=1, source_target_pairs={{0,256},{128,384},{256,0},{384,128},{1,257},{129,385},{257,1},{385... | collective-permute-start | bytes 1572872 | tf_op jit(solution)/shard_map/ppermute | solution.py:222
  19.3 53.0 %collective-permute-start.2 = (bf16[512,512]{1,0:T(8,128)(2,1)}, bf16[512,512]{1,0:T(8,128)(2,1)}, u32[]{:S(2)}, u32[]{:S(2)}) collective-permute-start(bf16[512,512]{1,0:T(8,128)(2,1)} %get-tuple-element.22), channel_id=1, source_target_pairs={{0,384},{128,0},{256,128},{384,256},{1,385},{129,1},{257,129},{385... | collective-permute-start | bytes 1572872 | tf_op jit(solution)/shard_map/ppermute | solution.py:222
  24.1 52.2 %all-to-all-start.2 = ((s32[128,1,8]{2,1,0:T(1,128)}), s32[128,1,8]{2,1,0:T(1,128)S(1)}, u32[]{:S(2)}, u32[]{:S(2)}) async-start(s32[128,1,8]{2,1,0:T(1,128)} %bitcast.9), calls=%async_computation.2 | async-start | bytes 131072 | tf_op jit(solution)/shard_map/all_to_all | solution.py:244
  41.0 50.4 %collective-permute-start.3 = (bf16[512,512]{1,0:T(8,128)(2,1)}, bf16[512,512]{1,0:T(8,128)(2,1)}, u32[]{:S(2)}, u32[]{:S(2)}) collective-permute-start(bf16[512,512]{1,0:T(8,128)(2,1)} %get-tuple-element.26), channel_id=1, source_target_pairs={{0,128},{128,256},{256,384},{384,0},{1,129},{129,257},{257,385},{3... | collective-permute-start | bytes 1572872 | tf_op jit(solution)/shard_map/ppermute | solution.py:222
  43.5 75.5 %collective-permute-start.4 = (bf16[512,512]{1,0:T(8,128)(2,1)}, bf16[512,512]{1,0:T(8,128)(2,1)}, u32[]{:S(2)}, u32[]{:S(2)}) collective-permute-start(bf16[512,512]{1,0:T(8,128)(2,1)} %get-tuple-element.27), channel_id=1, source_target_pairs={{0,256},{128,384},{256,0},{384,128},{1,257},{129,385},{257,1},{385... | collective-permute-start | bytes 1572872 | tf_op jit(solution)/shard_map/ppermute | solution.py:222
  46.2 72.7 %collective-permute-start.5 = (bf16[512,512]{1,0:T(8,128)(2,1)}, bf16[512,512]{1,0:T(8,128)(2,1)}, u32[]{:S(2)}, u32[]{:S(2)}) collective-permute-start(bf16[512,512]{1,0:T(8,128)(2,1)} %get-tuple-element.28), channel_id=1, source_target_pairs={{0,384},{128,0},{256,128},{384,256},{1,385},{129,1},{257,129},{385... | collective-permute-start | bytes 1572872 | tf_op jit(solution)/shard_map/ppermute | solution.py:222
  75.3 1.0 copy-start.1
  76.3 49.5 %all-to-all-start = ((bf16[128,8,512]{2,1,0:T(8,128)(2,1)}), bf16[128,8,512]{2,1,0:T(8,128)(2,1)S(1)}, u32[]{:S(2)}, u32[]{:S(2)}) async-start(bf16[128,8,512]{2,1,0:T(8,128)(2,1)} %bitcast.13), calls=%async_computation | async-start | bytes 2097152 | tf_op jit(solution)/shard_map/all_to_all | solution.py:228
  122.3 1.0 copy-start.2
  125.8 40.9 %all-to-all-start.1 = ((bf16[128,8,512]{2,1,0:T(8,128)(2,1)}), bf16[128,8,512]{2,1,0:T(8,128)(2,1)S(1)}, u32[]{:S(2)}, u32[]{:S(2)}) async-start(bf16[128,8,512]{2,1,0:T(8,128)(2,1)} %bitcast.14), calls=%async_computation.1 | async-start | bytes 2097152 | tf_op jit(solution)/shard_map/all_to_all | solution.py:228

commit v3 on v2

--- a/solution.py
+++ b/solution.py
@@ -132,7 +132,7 @@
         in_specs=[smem, smem, vmem, vmem] + [vmem] * len(left),
         out_specs=vmem,
         out_shape=jax.ShapeDtypeStruct((slots, rows), jnp.bfloat16),
-        compiler_params=pltpu.CompilerParams(vmem_limit_bytes=32 * 2**20),
+        compiler_params=pltpu.CompilerParams(vmem_limit_bytes=62 * 2**20),
         cost_estimate=pl.CostEstimate(
             flops=50_000_000_000, bytes_accessed=8 * size * size, transcendentals=0
         ),
@@ -199,7 +199,7 @@
             pltpu.SemaphoreType.DMA((len(arrived), TILES)),
             pltpu.SemaphoreType.DMA((TILES,)),
         ],
-        compiler_params=pltpu.CompilerParams(vmem_limit_bytes=32 * 2**20),
+        compiler_params=pltpu.CompilerParams(vmem_limit_bytes=62 * 2**20),
         cost_estimate=pl.CostEstimate(
             flops=3 * rows * wide, bytes_accessed=4 * rows * wide, transcendentals=0
         ),

time: 170 us -> 171 us (level)
  Pallas kernels: 15 us -> 18.2 us
    pallas_call x2, Pallas kernels: 6.32 us -> 9.91 us  [products(): pl.pallas_call(lambda *refs: products_kernel(chunk, *refs), in_specs=[sme...]
  transfers between devices with their start and end apart: 9 -> 9, of which waited for: 4 -> 4; matrix products, arithmetic and copies ran while one was open for 1% -> 1% of each run, Pallas kernels for 6% -> 7%
where the time goes in v3:
time: 171 us; the launch traced here: 170 us
  waiting for transfers between devices  78.5 us (46%)
  starting transfers between devices  70 us (41%)
  Pallas kernels  18.2 us (11%)
  local copies, waits for them, and re-layouts  2.18 us (1%)
    ppermute x6, waiting for transfers between devices, exchange(): lax.ppermute(block, 'row', [(i, (i + k + 1) % places) for i in range(plac...  47.1 us
    all_to_all x2, waiting for transfers between devices, to_owners(): lax.all_to_all(values, OWNERS, split_axis=0, concat_axis=0, tiled=True)  31.4 us
    ppermute x6, starting transfers between devices, exchange(): lax.ppermute(block, 'row', [(i, (i + k + 1) % places) for i in range(plac...  30.6 us
    all_to_all x2, starting transfers between devices, to_owners(): lax.all_to_all(values, OWNERS, split_axis=0, concat_axis=0, tiled=True)  26.1 us
    all_to_all x1, starting transfers between devices, shards(): lax.all_to_all(ids.reshape(clusters, capacity), OWNERS, split_axis=0, con...  13.3 us
    pallas_call x2, Pallas kernels, products(): pl.pallas_call(lambda *refs: products_kernel(chunk, *refs), in_specs=[sme...  9.91 us
    pallas_call x2, Pallas kernels, stage(): pl.pallas_call(lambda *refs: stage_kernel(chunk, *refs), in_specs=[pl.Blo...  5.3 us
  transfers between devices with their start and end apart: 9, of which 4 were waited for; matrix products, arithmetic and copies ran while one was open for 1% of the time, Pallas kernels for 7%

profile of v3, /device:TPU:1, one launch (start us, length us, event | category | flops | bytes accessed | tf_op | source)
XLA Modules:
  0.0 170.4 jit_solution(17748939646608186379)
XLA Ops:
  0.6 0.0 copy-start.2
  0.6 3.2 %stage.2 = (bf16[512,512]{1,0:T(8,128)(2,1)}, bf16[512,512]{1,0:T(8,128)(2,1)}, bf16[512,512]{1,0:T(8,128)(2,1)}) custom-call(s32[1,4]{1,0:T(1,128)} %refs_0_.6, s32[2,512]{1,0:T(2,128)} %bitcast.16, bf16[1,4,512,512]{3,2,1,0:T(8,128)(2,1)} %refs_3_.3), custom_call_target="tpu_custom_call" | custom-call | bytes 3145728 | tf_op jit(solution)/shard_map/stage/pallas_call | solution.py:77
  3.8 6.6 %collective-permute-start = (bf16[512,512]{1,0:T(8,128)(2,1)}, bf16[512,512]{1,0:T(8,128)(2,1)S(1)}, u32[]{:S(2)}, u32[]{:S(2)}) collective-permute-start(bf16[512,512]{1,0:T(8,128)(2,1)} %get-tuple-element.20), channel_id=1, source_target_pairs={{0,128},{128,256},{256,384},{384,0},{1,129},{129,257},{257,385},{3... | collective-permute-start | bytes 1572872 | tf_op jit(solution)/shard_map/ppermute | solution.py:222
  10.5 8.8 %collective-permute-start.1 = (bf16[512,512]{1,0:T(8,128)(2,1)}, bf16[512,512]{1,0:T(8,128)(2,1)S(1)}, u32[]{:S(2)}, u32[]{:S(2)}) collective-permute-start(bf16[512,512]{1,0:T(8,128)(2,1)} %get-tuple-element.21), channel_id=1, source_target_pairs={{0,256},{128,384},{256,0},{384,128},{1,257},{129,385},{257,1},{385... | collective-permute-start | bytes 1572872 | tf_op jit(solution)/shard_map/ppermute | solution.py:222
  19.3 3.4 %collective-permute-start.2 = (bf16[512,512]{1,0:T(8,128)(2,1)}, bf16[512,512]{1,0:T(8,128)(2,1)S(1)}, u32[]{:S(2)}, u32[]{:S(2)}) collective-permute-start(bf16[512,512]{1,0:T(8,128)(2,1)} %get-tuple-element.22), channel_id=1, source_target_pairs={{0,384},{128,0},{256,128},{384,256},{1,385},{129,1},{257,129},{385... | collective-permute-start | bytes 1572872 | tf_op jit(solution)/shard_map/ppermute | solution.py:222
  22.7 0.0 copy-done.2
  22.7 0.3 fusion
  23.0 0.0 copy-start.1
  23.0 0.4 select_reduce_fusion
  23.4 0.7 all_to_all.14
  24.1 13.3 %all-to-all-start.2 = ((s32[128,1,8]{2,1,0:T(1,128)}), s32[128,1,8]{2,1,0:T(1,128)S(1)}, u32[]{:S(2)}, u32[]{:S(2)}) async-start(s32[128,1,8]{2,1,0:T(1,128)} %bitcast.9), calls=%async_computation.2 | async-start | bytes 131072 | tf_op jit(solution)/shard_map/all_to_all | solution.py:244
  37.4 2.1 %stage.3 = (bf16[512,512]{1,0:T(8,128)(2,1)}, bf16[512,512]{1,0:T(8,128)(2,1)}, bf16[512,512]{1,0:T(8,128)(2,1)}) custom-call(s32[1,4]{1,0:T(1,128)} %refs_0_.6, s32[2,512]{1,0:T(2,128)} %bitcast.17, bf16[1,4,512,512]{3,2,1,0:T(8,128)(2,1)} %refs_3_.3), custom_call_target="tpu_custom_call" | custom-call | bytes 3145728 | tf_op jit(solution)/shard_map/stage/pallas_call | solution.py:77
  39.5 3.7 %collective-permute-start.3 = (bf16[512,512]{1,0:T(8,128)(2,1)}, bf16[512,512]{1,0:T(8,128)(2,1)}, u32[]{:S(2)}, u32[]{:S(2)}) collective-permute-start(bf16[512,512]{1,0:T(8,128)(2,1)} %get-tuple-element.26), channel_id=1, source_target_pairs={{0,128},{128,256},{256,384},{384,0},{1,129},{129,257},{257,385},{3... | collective-permute-start | bytes 1572872 | tf_op jit(solution)/shard_map/ppermute | solution.py:222
  43.3 2.9 %collective-permute-start.4 = (bf16[512,512]{1,0:T(8,128)(2,1)}, bf16[512,512]{1,0:T(8,128)(2,1)}, u32[]{:S(2)}, u32[]{:S(2)}) collective-permute-start(bf16[512,512]{1,0:T(8,128)(2,1)} %get-tuple-element.27), channel_id=1, source_target_pairs={{0,256},{128,384},{256,0},{384,128},{1,257},{129,385},{257,1},{385... | collective-permute-start | bytes 1572872 | tf_op jit(solution)/shard_map/ppermute | solution.py:222
  46.2 0.0 collective-permute-done.refs_4_
  46.2 0.0 copy-start.3
  46.2 5.2 %collective-permute-start.5 = (bf16[512,512]{1,0:T(8,128)(2,1)}, bf16[512,512]{1,0:T(8,128)(2,1)}, u32[]{:S(2)}, u32[]{:S(2)}) collective-permute-start(bf16[512,512]{1,0:T(8,128)(2,1)} %get-tuple-element.28), channel_id=1, source_target_pairs={{0,384},{128,0},{256,128},{384,256},{1,385},{129,1},{257,129},{385... | collective-permute-start | bytes 1572872 | tf_op jit(solution)/shard_map/ppermute | solution.py:222
  51.3 0.0 collective-permute-done.1.refs_5_
  51.4 0.0 copy-start.4
  51.4 20.9 %collective-permute-done.2.refs_6_ = bf16[512,512]{1,0:T(8,128)(2,1)S(1)} collective-permute-done((bf16[512,512]{1,0:T(8,128)(2,1)}, bf16[512,512]{1,0:T(8,128)(2,1)S(1)}, u32[]{:S(2)}, u32[]{:S(2)}) %collective-permute-start.2) | collective-permute-done | bytes 524320 | tf_op jit(solution)/shard_map/ppermute | solution.py:222
  72.3 0.0 copy-start.5
  72.3 0.0 copy-done.1
  72.3 0.0 copy-done.3
  72.3 0.0 copy-done.4
  72.3 0.8 copy-done.5
  73.1 5.0 %products.2 = bf16[1024,512]{1,0:T(8,128)(2,1)} custom-call(s32[1,4]{1,0:T(1,128)} %refs_0_.6, s32[2,512]{1,0:T(2,128)} %bitcast.18, s32[1,512]{1,0:T(1,128)} %bitcast.20, bf16[1,4,512,512]{3,2,1,0:T(8,128)(2,1)} %refs_3_.3, bf16[512,512]{1,0:T(8,128)(2,1)} %copy-done.3, bf16[512,512]{1,0:T(8,128)(2,1)} %copy-done.4, bf16[512,512]{1,0:T(8,128)(2,1)} %copy-done.5), custom_call_target="tpu_custom_call" | custom-call | flops 49999998976 | bytes 2097152 | tf_op jit(solution)/shard_map/products/pallas_call | solution.py:130
  78.1 0.0 all-to-all-done.2
  78.1 13.0 %all-to-all-start = ((bf16[128,8,512]{2,1,0:T(8,128)(2,1)}), bf16[128,8,512]{2,1,0:T(8,128)(2,1)S(1)}, u32[]{:S(2)}, u32[]{:S(2)}) async-start(bf16[128,8,512]{2,1,0:T(8,128)(2,1)} %bitcast.13), calls=%async_computation | async-start | bytes 2097152 | tf_op jit(solution)/shard_map/all_to_all | solution.py:228
  91.0 0.0 collective-permute-done.3.refs_4_
  91.1 26.1 %collective-permute-done.4.refs_5_ = bf16[512,512]{1,0:T(8,128)(2,1)} collective-permute-done((bf16[512,512]{1,0:T(8,128)(2,1)}, bf16[512,512]{1,0:T(8,128)(2,1)}, u32[]{:S(2)}, u32[]{:S(2)}) %collective-permute-start.4) | collective-permute-done | bytes 524320 | tf_op jit(solution)/shard_map/ppermute | solution.py:222
  117.2 0.0 collective-permute-done.5.refs_6_
  117.2 5.0 %products.3 = bf16[1024,512]{1,0:T(8,128)(2,1)} custom-call(s32[1,4]{1,0:T(1,128)} %refs_0_.6, s32[2,512]{1,0:T(2,128)} %bitcast.19, s32[1,512]{1,0:T(1,128)} %bitcast.21, bf16[1,4,512,512]{3,2,1,0:T(8,128)(2,1)} %refs_3_.3, bf16[512,512]{1,0:T(8,128)(2,1)} %collective-permute-done.3.refs_4_, bf16[512,512]{1,0:T(8,128)(2,1)} %collective-permute-done.4.refs_5_, ...), custom_call_target="tpu_custom_call" | custom-call | flops 49999998976 | bytes 2097152 | tf_op jit(solution)/shard_map/products/pallas_call | solution.py:130
  122.1 3.7 %all-to-all-done = bf16[128,8,512]{2,1,0:T(8,128)(2,1)S(1)} async-done(((bf16[128,8,512]{2,1,0:T(8,128)(2,1)}), bf16[128,8,512]{2,1,0:T(8,128)(2,1)S(1)}, u32[]{:S(2)}, u32[]{:S(2)}) %all-to-all-start) | async-done | bytes 1048608 | tf_op jit(solution)/shard_map/all_to_all | solution.py:228
  125.8 0.0 copy-start
  125.8 13.2 %all-to-all-start.1 = ((bf16[128,8,512]{2,1,0:T(8,128)(2,1)}), bf16[128,8,512]{2,1,0:T(8,128)(2,1)}, u32[]{:S(2)}, u32[]{:S(2)}) async-start(bf16[128,8,512]{2,1,0:T(8,128)(2,1)} %bitcast.14), calls=%async_computation.1 | async-start | bytes 2097152 | tf_op jit(solution)/shard_map/all_to_all | solution.py:228
  139.0 0.7 copy.10
  139.6 27.8 %all-to-all-done.1 = bf16[128,8,512]{2,1,0:T(8,128)(2,1)} async-done(((bf16[128,8,512]{2,1,0:T(8,128)(2,1)}), bf16[128,8,512]{2,1,0:T(8,128)(2,1)}, u32[]{:S(2)}, u32[]{:S(2)}) %all-to-all-start.1) | async-done | bytes 1048608 | tf_op jit(solution)/shard_map/all_to_all | solution.py:228
  167.4 0.0 copy-done
  167.4 3.0 %finish.1 = bf16[1024,1024]{1,0:T(8,128)(2,1)} custom-call(bf16[1024,512]{1,0:T(8,128)(2,1)} %bitcast.11, bf16[1024,512]{1,0:T(8,128)(2,1)} %bitcast.7.refs_1_), custom_call_target="tpu_custom_call" | custom-call | flops 3145728 | bytes 4194304 | tf_op jit(solution)/shard_map/finish/pallas_call | solution.py:191
  (2 shorter events, 0.0 us)
Async XLA Ops:
  0.6 22.0 %copy-start.2 = (s32[512,1]{0,1:T(1,128)S(1)}, s32[512,1]{0,1:T(1,128)}, u32[]{:S(2)}) copy-start(s32[512,1]{0,1:T(1,128)} %param.7) | copy-start | bytes 6148
  3.8 42.3 %collective-permute-start = (bf16[512,512]{1,0:T(8,128)(2,1)}, bf16[512,512]{1,0:T(8,128)(2,1)S(1)}, u32[]{:S(2)}, u32[]{:S(2)}) collective-permute-start(bf16[512,512]{1,0:T(8,128)(2,1)} %get-tuple-element.20), channel_id=1, source_target_pairs={{0,128},{128,256},{256,384},{384,0},{1,129},{129,257},{257,385},{3... | collective-permute-start | bytes 1572872 | tf_op jit(solution)/shard_map/ppermute | solution.py:222
  10.5 40.9 %collective-permute-start.1 = (bf16[512,512]{1,0:T(8,128)(2,1)}, bf16[512,512]{1,0:T(8,128)(2,1)S(1)}, u32[]{:S(2)}, u32[]{:S(2)}) collective-permute-start(bf16[512,512]{1,0:T(8,128)(2,1)} %get-tuple-element.21), channel_id=1, source_target_pairs={{0,256},{128,384},{256,0},{384,128},{1,257},{129,385},{257,1},{385... | collective-permute-start | bytes 1572872 | tf_op jit(solution)/shard_map/ppermute | solution.py:222
  19.3 53.0 %collective-permute-start.2 = (bf16[512,512]{1,0:T(8,128)(2,1)}, bf16[512,512]{1,0:T(8,128)(2,1)S(1)}, u32[]{:S(2)}, u32[]{:S(2)}) collective-permute-start(bf16[512,512]{1,0:T(8,128)(2,1)} %get-tuple-element.22), channel_id=1, source_target_pairs={{0,384},{128,0},{256,128},{384,256},{1,385},{129,1},{257,129},{385... | collective-permute-start | bytes 1572872 | tf_op jit(solution)/shard_map/ppermute | solution.py:222
  23.0 49.3 %copy-start.1 = (s32[512]{0:T(512)}, s32[512]{0:T(512)S(1)}, u32[]{:S(2)}) copy-start(s32[512]{0:T(512)S(1)} %convert_add_fusion) | copy-start | bytes 6148
  24.1 54.0 %all-to-all-start.2 = ((s32[128,1,8]{2,1,0:T(1,128)}), s32[128,1,8]{2,1,0:T(1,128)S(1)}, u32[]{:S(2)}, u32[]{:S(2)}) async-start(s32[128,1,8]{2,1,0:T(1,128)} %bitcast.9), calls=%async_computation.2 | async-start | bytes 131072 | tf_op jit(solution)/shard_map/all_to_all | solution.py:244
  39.5 51.5 %collective-permute-start.3 = (bf16[512,512]{1,0:T(8,128)(2,1)}, bf16[512,512]{1,0:T(8,128)(2,1)}, u32[]{:S(2)}, u32[]{:S(2)}) collective-permute-start(bf16[512,512]{1,0:T(8,128)(2,1)} %get-tuple-element.26), channel_id=1, source_target_pairs={{0,128},{128,256},{256,384},{384,0},{1,129},{129,257},{257,385},{3... | collective-permute-start | bytes 1572872 | tf_op jit(solution)/shard_map/ppermute | solution.py:222
  43.3 73.9 %collective-permute-start.4 = (bf16[512,512]{1,0:T(8,128)(2,1)}, bf16[512,512]{1,0:T(8,128)(2,1)}, u32[]{:S(2)}, u32[]{:S(2)}) collective-permute-start(bf16[512,512]{1,0:T(8,128)(2,1)} %get-tuple-element.27), channel_id=1, source_target_pairs={{0,256},{128,384},{256,0},{384,128},{1,257},{129,385},{257,1},{385... | collective-permute-start | bytes 1572872 | tf_op jit(solution)/shard_map/ppermute | solution.py:222
  46.2 26.1 %copy-start.3 = (bf16[512,512]{1,0:T(8,128)(2,1)}, bf16[512,512]{1,0:T(8,128)(2,1)S(1)}, u32[]{:S(2)}) copy-start(bf16[512,512]{1,0:T(8,128)(2,1)S(1)} %collective-permute-done.refs_4_) | copy-start | bytes 1572868
  46.2 71.0 %collective-permute-start.5 = (bf16[512,512]{1,0:T(8,128)(2,1)}, bf16[512,512]{1,0:T(8,128)(2,1)}, u32[]{:S(2)}, u32[]{:S(2)}) collective-permute-start(bf16[512,512]{1,0:T(8,128)(2,1)} %get-tuple-element.28), channel_id=1, source_target_pairs={{0,384},{128,0},{256,128},{384,256},{1,385},{129,1},{257,129},{385... | collective-permute-start | bytes 1572872 | tf_op jit(solution)/shard_map/ppermute | solution.py:222
  51.4 21.0 %copy-start.4 = (bf16[512,512]{1,0:T(8,128)(2,1)}, bf16[512,512]{1,0:T(8,128)(2,1)S(1)}, u32[]{:S(2)}) copy-start(bf16[512,512]{1,0:T(8,128)(2,1)S(1)} %collective-permute-done.1.refs_5_) | copy-start | bytes 1572868
  72.3 0.8 copy-start.5
  78.1 47.7 %all-to-all-start = ((bf16[128,8,512]{2,1,0:T(8,128)(2,1)}), bf16[128,8,512]{2,1,0:T(8,128)(2,1)S(1)}, u32[]{:S(2)}, u32[]{:S(2)}) async-start(bf16[128,8,512]{2,1,0:T(8,128)(2,1)} %bitcast.13), calls=%async_computation | async-start | bytes 2097152 | tf_op jit(solution)/shard_map/all_to_all | solution.py:228
  125.8 41.6 %copy-start = (bf16[128,8,512]{2,1,0:T(8,128)(2,1)}, bf16[128,8,512]{2,1,0:T(8,128)(2,1)S(1)}, u32[]{:S(2)}) copy-start(bf16[128,8,512]{2,1,0:T(8,128)(2,1)S(1)} %all-to-all-done) | copy-start | bytes 3145732
  125.8 41.6 %all-to-all-start.1 = ((bf16[128,8,512]{2,1,0:T(8,128)(2,1)}), bf16[128,8,512]{2,1,0:T(8,128)(2,1)}, u32[]{:S(2)}, u32[]{:S(2)}) async-start(bf16[128,8,512]{2,1,0:T(8,128)(2,1)} %bitcast.14), calls=%async_computation.1 | async-start | bytes 2097152 | tf_op jit(solution)/shard_map/all_to_all | solution.py:228
